TPU v7x, 32 devices: a whole 2x2x4 slice. The times are simulated.
32 devices in a mesh: dp: 2 (over x), seq: 4 (over z), expert: 4 (over y, core).
Axes of the slice: x: 2, y: 2, z: 4, core: 2. Of those that a mesh axis runs over, the one named last changes fastest.
Arguments:
- tokens: bfloat16 [8192, 2048], P(('dp', 'seq', 'expert')), may hold values from -6 to 6
- grad_out: bfloat16 [8192, 2048], P(('dp', 'seq', 'expert')), may hold values from -6 to 6
- route_weights: bfloat16 [8192, 2], P(('dp', 'seq', 'expert')), may hold values from 0.099609375 to 1
- expert_ids: int32 [8192, 2], P(('dp', 'seq', 'expert')), may hold values from 0 to 63, as said below
- route_slots: int32 [8192, 2], P(('dp', 'seq', 'expert')), may hold values from 0 to 7, as said below
- w_gate: bfloat16 [64, 2048, 1024], P(('seq', 'expert')), may hold values from -0.125 to 0.125
- w_up: bfloat16 [64, 2048, 1024], P(('seq', 'expert')), may hold values from -0.125 to 0.125
- w_down: bfloat16 [64, 2048, 1024], P(('seq', 'expert')), may hold values from -0.1875 to 0.1875
Outputs:
- grad_tokens: bfloat16 [8192, 2048], P(('dp', 'seq', 'expert'))
- grad_gate: bfloat16 [64, 2048, 1024], P(('seq', 'expert'), 'dp')
- grad_up: bfloat16 [64, 2048, 1024], P(('seq', 'expert'), 'dp')
- grad_down: bfloat16 [64, 2048, 1024], P(('seq', 'expert'), 'dp')
Inputs may be any that keep to these rules, and one draw needn't show every extreme that they name: `expert_ids`: in every block of 256 cells, a cell's two experts differ, each expert is named by exactly 8 of the block's routes, and the experts fall into two halves drawn from the seed with each cell naming one expert of each half. `route_slots`: within a block the routes to one expert take the slots 0 to 7, each once.
All inputs are finite; a program needn't handle non-finite values.
Results may differ from a plain program's by a relative error of at most 0.0065.
Values may be sent and summed in bfloat16 or wider, within the bound.
A program may use at most 192 MiB of HBM per device.

v0:
```python
import jax
import jax.numpy as jnp
from jax import lax
from jax.sharding import PartitionSpec as P

E = 64


def per_device(tokens, grad_out, route_weights, expert_ids, route_slots, w_gate, w_up, w_down):
    seq_count = lax.axis_size("seq")
    exp_count = lax.axis_size("expert")
    group = seq_count * exp_count
    exp_local = w_gate.shape[0]
    cell_count = tokens.shape[0]
    width = tokens.shape[1]
    slot_count = 2 * cell_count // E
    position = expert_ids * slot_count + route_slots
    cells = jnp.arange(cell_count, dtype=jnp.int32)
    table = (
        jnp.zeros((E * slot_count,), jnp.int32)
        .at[position]
        .set(jnp.broadcast_to(cells[:, None], (cell_count, 2)))
    )
    weight_table = jnp.zeros((E * slot_count,), jnp.bfloat16).at[position].set(route_weights)
    send_x = tokens[table].reshape(group, exp_local, slot_count, width)
    send_g = grad_out[table].reshape(group, exp_local, slot_count, width)
    send_c = weight_table.reshape(group, exp_local, slot_count)
    recv_x, recv_g, recv_c = (
        lax.all_to_all(send_x, ("seq", "expert"), split_axis=0, concat_axis=0, tiled=True),
        lax.all_to_all(send_g, ("seq", "expert"), split_axis=0, concat_axis=0, tiled=True),
        lax.all_to_all(send_c, ("seq", "expert"), split_axis=0, concat_axis=0, tiled=True),
    )
    gate_pre = jnp.einsum("gesd,edf->gesf", recv_x, w_gate, preferred_element_type=jnp.float32)
    up_pre = jnp.einsum("gesd,edf->gesf", recv_x, w_up, preferred_element_type=jnp.float32)
    gate_sig = jax.nn.sigmoid(gate_pre)
    silu_g = gate_pre * gate_sig
    act = (silu_g * up_pre).astype(jnp.bfloat16)
    route_grad = (recv_c.astype(jnp.float32)[..., None] * recv_g.astype(jnp.float32)).astype(
        jnp.bfloat16
    )
    act_grad = jnp.einsum("gesd,edf->gesf", route_grad, w_down, preferred_element_type=jnp.float32)
    gate_grad = (act_grad * up_pre * gate_sig * (1.0 + gate_pre * (1.0 - gate_sig))).astype(
        jnp.bfloat16
    )
    up_grad = (act_grad * silu_g).astype(jnp.bfloat16)
    acc_gate = jnp.einsum("gesd,gesf->edf", recv_x, gate_grad, preferred_element_type=jnp.float32)
    acc_up = jnp.einsum("gesd,gesf->edf", recv_x, up_grad, preferred_element_type=jnp.float32)
    acc_down = jnp.einsum("gesd,gesf->edf", route_grad, act, preferred_element_type=jnp.float32)
    back = jnp.einsum("gesf,edf->gesd", gate_grad, w_gate, preferred_element_type=jnp.float32)
    back = (
        back + jnp.einsum("gesf,edf->gesd", up_grad, w_up, preferred_element_type=jnp.float32)
    ).astype(jnp.bfloat16)
    returned = lax.all_to_all(back, ("seq", "expert"), split_axis=0, concat_axis=0, tiled=True)
    returned = returned.reshape(E * slot_count, width)
    grad_tokens = (
        returned[position[:, 0]].astype(jnp.float32) + returned[position[:, 1]].astype(jnp.float32)
    ).astype(jnp.bfloat16)
    grad_gate, grad_up, grad_down = (
        lax.psum_scatter(
            acc_gate.astype(jnp.bfloat16), "dp", scatter_dimension=1, tiled=True
        ).astype(jnp.float32),
        lax.psum_scatter(acc_up.astype(jnp.bfloat16), "dp", scatter_dimension=1, tiled=True).astype(
            jnp.float32
        ),
        lax.psum_scatter(
            acc_down.astype(jnp.bfloat16), "dp", scatter_dimension=1, tiled=True
        ).astype(jnp.float32),
    )
    return (
        grad_tokens,
        grad_gate.astype(jnp.bfloat16),
        grad_up.astype(jnp.bfloat16),
        grad_down.astype(jnp.bfloat16),
    )


def solution(mesh):
    return jax.shard_map(
        per_device,
        mesh=mesh,
        in_specs=(
            P(("dp", "seq", "expert"), None),
            P(("dp", "seq", "expert"), None),
            P(("dp", "seq", "expert"), None),
            P(("dp", "seq", "expert"), None),
            P(("dp", "seq", "expert"), None),
            P(("seq", "expert"), None, None),
            P(("seq", "expert"), None, None),
            P(("seq", "expert"), None, None),
        ),
        out_specs=(
            P(("dp", "seq", "expert"), None),
            P(("seq", "expert"), "dp", None),
            P(("seq", "expert"), "dp", None),
            P(("seq", "expert"), "dp", None),
        ),
        check_vma=False,
    )
```

profile of v0, /device:TPU:29, one launch (start us, length us, event | category | flops | bytes accessed | tf_op | source)
XLA Modules:
  0.0 744.3 jit_solution(5247103767674552189)
XLA Ops:
  7.2 0.0 copy-start
  7.2 0.9 copy.32
  8.1 0.1 reshape.61
  8.2 1.3 compare_select_fusion
  9.5 0.1 copy.31
  9.7 0.1 reshape.59
  9.8 3.8 scatter_custom_fusion
  13.6 0.7 reshape.21
  14.3 6.3 all-to-all-start
  20.6 0.1 reshape.69
  20.8 2.4 scatter_custom_fusion.1
  23.3 0.0 copy-done
  23.3 3.3 gather_fusion.1
  26.5 0.0 all-to-all-done
  26.6 0.0 copy-start.2
  26.6 6.2 all-to-all-start.2
  32.7 0.0 copy-done.2
  32.7 3.3 gather_fusion
  36.0 43.2 %all-to-all-done.2 = bf16[16,4,8,2048]{3,2,1,0:T(8,128)(2,1)S(1)} async-done(((bf16[16,4,8,2048]{3,2,1,0:T(8,128)(2,1)}), bf16[16,4,8,2048]{3,2,1,0:T(8,128)(2,1)S(1)}, u32[]{:S(2)}, u32[]{:S(2)}) %all-to-all-start.2) | async-done | bytes 2097184 | tf_op jit(solution)/shard_map/all_to_all | solution.py:29
  79.2 5.9 all-to-all-start.1
  85.0 0.2 reduce-scatter.8.cloned.1.call-start
  85.3 9.4 %fusion.2 = f32[4,16,8,1024]{3,2,1,0:T(8,128)} fusion(bf16[4,2048,1024]{2,1,0:T(8,128)(2,1)} %param.13, bf16[16,4,8,2048]{3,2,1,0:T(8,128)(2,1)S(1)} %all-to-all-done.2), kind=kOutput, calls=%fused_computation.11 | convolution fusion | flops 2147483648 | bytes 20971520 | tf_op jit(solution)/shard_map/gesd,edf->gesf/dot_general | solution.py:33
  94.7 36.9 %all-to-all-done.1 = bf16[16,4,8,2048]{3,2,1,0:T(8,128)(2,1)} async-done(((bf16[16,4,8,2048]{3,2,1,0:T(8,128)(2,1)}), bf16[16,4,8,2048]{3,2,1,0:T(8,128)(2,1)}, u32[]{:S(2)}, u32[]{:S(2)}) %all-to-all-start.1) | async-done | bytes 2097184 | tf_op jit(solution)/shard_map/all_to_all | solution.py:30
  131.6 8.9 %fusion.4 = f32[4,16,8,1024]{3,2,1,0:T(8,128)S(1)} fusion(bf16[4,2048,1024]{2,1,0:T(8,128)(2,1)} %param.15, bf16[16,4,8,2048]{3,2,1,0:T(8,128)(2,1)} %all-to-all-done.1, f32[16,4,8]{2,1,0:T(4,128)S(1)} %convert_element_type.48), kind=kOutput, calls=%fused_computation.13 | convolution fusion | flops 2150629376 | bytes 20973568 | tf_op jit(solution)/shard_map/gesd,edf->gesf/dot_general | solution.py:41
  140.5 0.0 copy-done.3
  140.5 10.9 %fusion.22 = (bf16[16,4,8,1024]{3,2,0,1:T(8,128)(2,1)}, bf16[16,4,8,1024]{3,2,0,1:T(8,128)(2,1)}, bf16[16,4,8,1024]{3,2,0,1:T(8,128)(2,1)S(1)}) fusion(f32[4,16,8,1024]{3,2,1,0:T(8,128)S(1)} %copy-done.3, f32[4,16,8,1024]{3,2,1,0:T(8,128)S(1)} %fusion.4, bf16[4,2048,1024]{2,1,0:T(8,128)(2,1)} %param.14, bf16[16,4,8,2048]{3,2,1,0:T(8,128)(2,1)S(1)} %all-to-all-done.2), kind=kOutput, calls=%fused_computation.34 | convolution fusion | flops 2155347968 | bytes 26214400 | tf_op jit(solution)/shard_map/gesd,edf->gesf/dot_general | solution.py:34
  151.4 12.4 %bitcast_convert_fusion = bf16[4,2048,1024]{2,1,0:T(8,128)(2,1)} fusion(bf16[16,4,8,1024]{3,2,0,1:T(8,128)(2,1)} %get-tuple-element.6, bf16[16,4,8,2048]{3,2,1,0:T(8,128)(2,1)} %all-to-all-done.1, f32[16,4,8]{2,1,0:T(4,128)S(1)} %convert_element_type.48), kind=kOutput, calls=%fused_computation.6 | convolution fusion | flops 2159017984 | bytes 19924992 | tf_op jit(solution)/shard_map/gesd,gesf->edf/dot_general | solution.py:48
  163.9 0.0 reduce-scatter.8.cloned.1.call-update
  163.9 0.0 reduce-scatter.6.cloned.1.call-start
  163.9 8.4 %bitcast_convert_fusion.1 = bf16[4,2048,1024]{2,1,0:T(8,128)(2,1)} fusion(bf16[16,4,8,2048]{3,2,1,0:T(8,128)(2,1)S(1)} %all-to-all-done.2, bf16[16,4,8,1024]{3,2,0,1:T(8,128)(2,1)S(1)} %get-tuple-element.8), kind=kOutput, calls=%fused_computation.7 | convolution fusion | flops 2155872256 | bytes 19922944 | tf_op jit(solution)/shard_map/gesd,gesf->edf/dot_general | solution.py:47
  172.3 0.0 reduce-scatter.6.cloned.1.call-update
  172.4 0.0 reduce-scatter.4.cloned.1.call-start
  172.4 9.6 %bitcast_convert_fusion.2 = bf16[4,2048,1024]{2,1,0:T(8,128)(2,1)} fusion(bf16[16,4,8,2048]{3,2,1,0:T(8,128)(2,1)S(1)} %all-to-all-done.2, bf16[16,4,8,1024]{3,2,0,1:T(8,128)(2,1)} %get-tuple-element.7), kind=kOutput, calls=%fused_computation.8 | convolution fusion | flops 2155872256 | bytes 19922944 | tf_op jit(solution)/shard_map/gesd,gesf->edf/dot_general | solution.py:46
  182.0 0.0 reduce-scatter.4.cloned.1.call-update
  182.0 1.2 copy-done.4
  183.2 13.7 %fusion = f32[4,16,8,2048]{3,2,1,0:T(8,128)} fusion(bf16[16,4,8,1024]{3,2,0,1:T(8,128)(2,1)S(1)} %copy-done.4, bf16[4,2048,1024]{2,1,0:T(8,128)(2,1)} %param.13), kind=kOutput, calls=%fused_computation.9 | convolution fusion | flops 2147483648 | bytes 22020096 | tf_op jit(solution)/shard_map/gesf,edf->gesd/dot_general | solution.py:49
  196.9 10.1 %fusion.12 = bf16[16,4,8,2048]{3,2,0,1:T(8,128)(2,1)S(1)} fusion(f32[4,16,8,2048]{3,2,1,0:T(8,128)} %fusion, bf16[16,4,8,1024]{3,2,0,1:T(8,128)(2,1)S(1)} %get-tuple-element.8, bf16[4,2048,1024]{2,1,0:T(8,128)(2,1)} %param.14), kind=kOutput, calls=%fused_computation.21 | convolution fusion | flops 2149580800 | bytes 24117248 | tf_op jit(solution)/shard_map/gesf,edf->gesd/dot_general | solution.py:51
  207.0 1.6 copy.36
  208.6 6.1 all-to-all-start.3
  214.7 0.0 copy-done.5
  214.7 46.4 %all-to-all-done.3 = bf16[16,4,8,2048]{3,2,1,0:T(8,128)(2,1)S(1)} async-done(((bf16[16,4,8,2048]{3,2,1,0:T(8,128)(2,1)}), bf16[16,4,8,2048]{3,2,1,0:T(8,128)(2,1)S(1)}, u32[]{:S(2)}, u32[]{:S(2)}) %all-to-all-start.3) | async-done | bytes 2097184 | tf_op jit(solution)/shard_map/all_to_all | solution.py:53
  261.1 2.3 gather_fusion.3
  263.5 2.4 gather_fusion.2
  265.8 2.9 add_convert_fusion.1
  268.7 84.9 %reduce-scatter.8.cloned.1.call-done = bf16[4,1024,1024]{2,1,0:T(8,128)(2,1)} async-done(((bf16[4,2048,1024]{2,1,0:T(8,128)(2,1)}), bf16[4,1024,1024]{2,1,0:T(8,128)(2,1)}) %reduce-scatter.8.cloned.1.call-update) | async-done | bytes 8388624 | tf_op jit(solution)/shard_map/reduce_scatter | solution.py:65
  353.6 192.2 %reduce-scatter.6.cloned.1.call-done = bf16[4,1024,1024]{2,1,0:T(8,128)(2,1)} async-done(((bf16[4,2048,1024]{2,1,0:T(8,128)(2,1)}), bf16[4,1024,1024]{2,1,0:T(8,128)(2,1)}) %reduce-scatter.6.cloned.1.call-update) | async-done | bytes 8388624 | tf_op jit(solution)/shard_map/reduce_scatter | solution.py:62
  545.8 192.0 %reduce-scatter.4.cloned.1.call-done = bf16[4,1024,1024]{2,1,0:T(8,128)(2,1)} async-done(((bf16[4,2048,1024]{2,1,0:T(8,128)(2,1)}), bf16[4,1024,1024]{2,1,0:T(8,128)(2,1)}) %reduce-scatter.4.cloned.1.call-update) | async-done | bytes 8388624 | tf_op jit(solution)/shard_map/reduce_scatter | solution.py:59
  737.8 0.0 copy-done.1
  (11 shorter events, 0.1 us)
Async XLA Ops:
  7.2 16.1 %copy-start = (bf16[256,2048]{1,0:T(8,128)(2,1)S(1)}, bf16[256,2048]{1,0:T(8,128)(2,1)}, u32[]{:S(2)}) copy-start(bf16[256,2048]{1,0:T(8,128)(2,1)} %param.8) | copy-start | bytes 3145732
  14.3 12.3 %all-to-all-start = ((bf16[16,4,8]{2,1,0:T(4,128)(2,1)}), bf16[16,4,8]{2,1,0:T(4,128)(2,1)S(1)}, u32[]{:S(2)}, u32[]{:S(2)}) async-start(bf16[16,4,8]{2,1,0:T(4,128)(2,1)} %reshape.21), calls=%async_computation | async-start | bytes 32768 | tf_op jit(solution)/shard_map/all_to_all | solution.py:31
  26.6 6.2 copy-start.2
  26.6 52.6 %all-to-all-start.2 = ((bf16[16,4,8,2048]{3,2,1,0:T(8,128)(2,1)}), bf16[16,4,8,2048]{3,2,1,0:T(8,128)(2,1)S(1)}, u32[]{:S(2)}, u32[]{:S(2)}) async-start(bf16[16,4,8,2048]{3,2,1,0:T(8,128)(2,1)} %bitcast.86), calls=%async_computation.2 | async-start | bytes 4194304 | tf_op jit(solution)/shard_map/all_to_all | solution.py:29
  79.2 52.4 %all-to-all-start.1 = ((bf16[16,4,8,2048]{3,2,1,0:T(8,128)(2,1)}), bf16[16,4,8,2048]{3,2,1,0:T(8,128)(2,1)}, u32[]{:S(2)}, u32[]{:S(2)}) async-start(bf16[16,4,8,2048]{3,2,1,0:T(8,128)(2,1)} %bitcast.85), calls=%async_computation.1 | async-start | bytes 4194304 | tf_op jit(solution)/shard_map/all_to_all | solution.py:30
  85.0 268.6 %reduce-scatter.8.cloned.1.call-start = ((), (), s32[]{:S(2)}) async-start(), calls=%async_computation.9 | async-start | bytes 25165824 | tf_op jit(solution)/shard_map/reduce_scatter | solution.py:65
  131.6 8.9 %copy-start.3 = (f32[4,16,8,1024]{3,2,1,0:T(8,128)S(1)}, f32[4,16,8,1024]{3,2,1,0:T(8,128)}, u32[]{:S(2)}) copy-start(f32[4,16,8,1024]{3,2,1,0:T(8,128)} %fusion.2) | copy-start | bytes 6291460
  163.9 381.9 %reduce-scatter.6.cloned.1.call-start = ((), (), s32[]{:S(2)}) async-start(), calls=%async_computation.8 | async-start | bytes 25165824 | tf_op jit(solution)/shard_map/reduce_scatter | solution.py:62
  172.4 565.4 %reduce-scatter.4.cloned.1.call-start = ((), (), s32[]{:S(2)}) async-start(), calls=%async_computation.7 | async-start | bytes 25165824 | tf_op jit(solution)/shard_map/reduce_scatter | solution.py:59
  182.0 1.2 copy-start.4
  208.6 6.1 copy-start.5
  208.6 52.5 %all-to-all-start.3 = ((bf16[16,4,8,2048]{3,2,1,0:T(8,128)(2,1)}), bf16[16,4,8,2048]{3,2,1,0:T(8,128)(2,1)S(1)}, u32[]{:S(2)}, u32[]{:S(2)}) async-start(bf16[16,4,8,2048]{3,2,1,0:T(8,128)(2,1)} %copy.36), calls=%async_computation.3 | async-start | bytes 4194304 | tf_op jit(solution)/shard_map/all_to_all | solution.py:53
  263.5 474.4 %copy-start.1 = (bf16[256,2048]{1,0:T(8,128)(2,1)S(1)}, bf16[256,2048]{1,0:T(8,128)(2,1)}, u32[]{:S(2)}) copy-start(bf16[256,2048]{1,0:T(8,128)(2,1)} %param.8) | copy-start | bytes 3145732
Sparse Core Ops, SparseCore 0:
  164.0 189.5 reduce-scatter.7
  356.6 189.1 reduce-scatter.5
  548.7 189.0 reduce-scatter.3
where the time goes:
time: 747 us; the launch traced here: 744 us
  waiting for transfers between devices  596 us (80%)
  matrix products  83.5 us (11%)
  starting transfers between devices  24.7 us (3%)
  local copies, waits for them, and re-layouts  22.4 us (3%)
  between operations  13.9 us (2%)
    reduce_scatter x1, waiting for transfers between devices, per_device(): lax.psum_scatter(acc_up.astype(jnp.bfloat16), 'dp', scatter_dimension=1,...  192 us
    reduce_scatter x1, waiting for transfers between devices, per_device(): lax.psum_scatter(acc_gate.astype(jnp.bfloat16), 'dp', scatter_dimension=1...  192 us
    reduce_scatter x1, waiting for transfers between devices, per_device(): lax.psum_scatter(acc_down.astype(jnp.bfloat16), 'dp', scatter_dimension=1...  84.9 us
    all_to_all x1, waiting for transfers between devices, per_device(): lax.all_to_all(back, ('seq', 'expert'), split_axis=0, concat_axis=0, tile...  46.4 us
    all_to_all x1, waiting for transfers between devices, per_device(): lax.all_to_all(send_x, ('seq', 'expert'), split_axis=0, concat_axis=0, ti...  43.2 us
    all_to_all x1, waiting for transfers between devices, per_device(): lax.all_to_all(send_g, ('seq', 'expert'), split_axis=0, concat_axis=0, ti...  36.9 us
  transfers between devices with their start and end apart: 7, of which 6 were waited for; matrix products, arithmetic and copies ran while one was open for 9% of the time, Pallas kernels for 0%

commit v1 on v0

v1 whole, which is shorter than its diff:
```python
import jax
import jax.numpy as jnp
from jax import lax
from jax.sharding import PartitionSpec as P

E = 64
BF = jnp.bfloat16
F32 = jnp.float32


def per_device(tokens, grad_out, route_weights, expert_ids, route_slots, w_gate, w_up, w_down):
    group = lax.axis_size("seq") * lax.axis_size("expert")
    el, width, ff = w_gate.shape
    cells = tokens.shape[0]
    slots = 2 * cells // E
    half = width // 2
    rows = group * slots
    dp = lax.axis_index("dp")
    position = expert_ids * slots + route_slots
    place = jnp.arange(E * slots, dtype=jnp.int32)[:, None]
    hit0 = (position[:, 0][None, :] == place).astype(BF)
    hit1 = (position[:, 1][None, :] == place).astype(BF)
    pick = hit0 + hit1
    weigh = hit0 * route_weights[:, 0][None, :] + hit1 * route_weights[:, 1][None, :]
    send_x = jnp.dot(pick, tokens, preferred_element_type=F32).astype(BF)
    send_g = jnp.dot(weigh, grad_out, preferred_element_type=F32).astype(BF)
    send_x = send_x.reshape(group, el, slots, width)
    send_g = send_g.reshape(group, el, slots, width)
    axes = ("seq", "expert")
    x = lax.all_to_all(send_x, axes, split_axis=0, concat_axis=0, tiled=True)
    g = lax.all_to_all(send_g, axes, split_axis=0, concat_axis=0, tiled=True)
    x = x.transpose(1, 0, 2, 3).reshape(el, rows, width)
    g = g.transpose(1, 0, 2, 3).reshape(el, rows, width)
    swap = [(0, 1), (1, 0)]
    far_x = lax.ppermute(lax.dynamic_slice_in_dim(x, (1 - dp) * half, half, 2), "dp", swap)
    far_g = lax.ppermute(lax.dynamic_slice_in_dim(g, (1 - dp) * half, half, 2), "dp", swap)
    my_x = lax.dynamic_slice_in_dim(x, dp * half, half, 2)
    my_g = lax.dynamic_slice_in_dim(g, dp * half, half, 2)
    gate_pre = jnp.einsum("erd,edf->erf", x, w_gate, preferred_element_type=F32)
    up_pre = jnp.einsum("erd,edf->erf", x, w_up, preferred_element_type=F32)
    act_grad = jnp.einsum("erd,edf->erf", g, w_down, preferred_element_type=F32)
    sig = jax.nn.sigmoid(gate_pre)
    silu = gate_pre * sig
    act = (silu * up_pre).astype(BF)
    gate_grad = (act_grad * up_pre * sig * (1.0 + gate_pre * (1.0 - sig))).astype(BF)
    up_grad = (act_grad * silu).astype(BF)
    far_a = lax.ppermute(act, "dp", swap)
    far_gg = lax.ppermute(gate_grad, "dp", swap)
    far_ug = lax.ppermute(up_grad, "dp", swap)
    back = jnp.einsum("erf,edf->erd", gate_grad, w_gate, preferred_element_type=F32)
    back = back + jnp.einsum("erf,edf->erd", up_grad, w_up, preferred_element_type=F32)
    back = back.astype(BF).reshape(el, group, slots, width).transpose(1, 0, 2, 3)
    returned = lax.all_to_all(back, axes, split_axis=0, concat_axis=0, tiled=True)
    returned = returned.reshape(E * slots, width)
    grad_tokens = jnp.einsum("pt,pd->td", pick, returned, preferred_element_type=F32).astype(BF)

    def wgrad(a0, a1, b0, b1):
        a = jnp.concatenate([a0, a1], 1)
        b = jnp.concatenate([b0, b1], 1)
        return jnp.einsum("erd,erf->edf", a, b, preferred_element_type=F32).astype(BF)

    return (
        grad_tokens,
        wgrad(my_x, far_x, gate_grad, far_gg),
        wgrad(my_x, far_x, up_grad, far_ug),
        wgrad(my_g, far_g, act, far_a),
    )


def solution(mesh):
    cell = P(("dp", "seq", "expert"), None)
    held = P(("seq", "expert"), None, None)
    grad = P(("seq", "expert"), "dp", None)
    return jax.shard_map(
        per_device,
        mesh=mesh,
        in_specs=(cell,) * 5 + (held,) * 3,
        out_specs=(cell, grad, grad, grad),
        check_vma=False,
    )
```

time: 747 us -> 286 us (0.38)
  waiting for transfers between devices: 596 us -> 180 us
  local copies, waits for them, and re-layouts: 22.4 us -> 5.43 us
  between operations: 13.9 us -> 0.73 us
  matrix products: 83.5 us -> 75.2 us
    reduce_scatter x3 -> x0, waiting for transfers between devices: 469 us -> none  [the longest x1 192 us: per_device(): lax.psum_scatter(acc_up.astype(jnp.bfloat16), 'dp', scatter_dimension=1,...]
    ppermute x0 -> x5, waiting for transfers between devices: none -> 98.2 us  [the longest x1 62.7 us: per_device(): lax.ppermute(lax.dynamic_slice_in_dim(x, (1 - dp) * half, half, 2), 'dp',...]
    all_to_all x4 -> x3, waiting for transfers between devices: 126 us -> 81.5 us  [the longest x1 44.4 us: per_device(): g = lax.all_to_all(send_g, axes, split_axis=0, concat_axis=0, tiled=True)]
    gather x4 -> x0, local copies, waits for them, and re-layouts: 11.2 us -> none  [the longest x1 3.28 us: per_device(): send_x = tokens[table].reshape(group, exp_local, slot_count, width)]
    dot_general x8 -> x11, matrix products: 83.5 us -> 75.2 us  [the longest x3 14.1 us: wgrad(): jnp.einsum('erd,erf->edf', a, b, preferred_element_type=F32).astype(BF)]
    all_to_all x4 -> x3, starting transfers between devices: 24.4 us -> 18.2 us  [the longest x1 6.46 us: per_device(): g = lax.all_to_all(send_g, axes, split_axis=0, concat_axis=0, tiled=True)]
  transfers between devices with their start and end apart: 7 -> 8, of which waited for: 6 -> 5; matrix products, arithmetic and copies ran while one was open for 9% -> 10% of each run, Pallas kernels for 0% -> 0%
where the time goes in v1:
time: 286 us; the launch traced here: 284 us
  waiting for transfers between devices  180 us (63%)
  matrix products  75.2 us (26%)
  starting transfers between devices  21.8 us (8%)
  local copies, waits for them, and re-layouts  5.43 us (2%)
    ppermute x1, waiting for transfers between devices, per_device(): lax.ppermute(lax.dynamic_slice_in_dim(x, (1 - dp) * half, half, 2), 'dp',...  62.7 us
    all_to_all x1, waiting for transfers between devices, per_device(): g = lax.all_to_all(send_g, axes, split_axis=0, concat_axis=0, tiled=True)  44.4 us
    all_to_all x1, waiting for transfers between devices, per_device(): x = lax.all_to_all(send_x, axes, split_axis=0, concat_axis=0, tiled=True)  37.1 us
    ppermute x1, waiting for transfers between devices, per_device(): far_a = lax.ppermute(act, 'dp', swap)  22.5 us
    dot_general x3, matrix products, wgrad(): jnp.einsum('erd,erf->edf', a, b, preferred_element_type=F32).astype(BF)  14.1 us
    dot_general x1, matrix products, per_device(): jnp.einsum('erf,edf->erd', gate_grad, w_gate, preferred_element_type=F32)  13.4 us
    ppermute x1, waiting for transfers between devices, per_device(): lax.ppermute(lax.dynamic_slice_in_dim(g, (1 - dp) * half, half, 2), 'dp',...  13 us
    dot_general x1, matrix products, per_device(): up_pre = jnp.einsum('erd,edf->erf', x, w_up, preferred_element_type=F32)  11.7 us
  transfers between devices with their start and end apart: 8, of which 5 were waited for; matrix products, arithmetic and copies ran while one was open for 10% of the time, Pallas kernels for 0%

profile of v1, /device:TPU:29, one launch (start us, length us, event | category | flops | bytes accessed | tf_op | source)
XLA Modules:
  0.0 283.6 jit_solution(6626177561305773425)
XLA Ops:
  0.6 0.0 copy-start
  0.6 0.8 slice_reduce_fusion.1
  1.5 0.7 multiply_add_fusion
  2.2 0.0 copy-done
  2.2 2.0 convolution_convert_fusion.4
  4.2 0.0 copy-start.4
  4.2 6.5 %all-to-all-start = ((bf16[16,4,8,2048]{3,2,1,0:T(8,128)(2,1)}), bf16[16,4,8,2048]{3,2,1,0:T(8,128)(2,1)S(1)}, u32[]{:S(2)}, u32[]{:S(2)}) async-start(bf16[16,4,8,2048]{3,2,1,0:T(8,128)(2,1)} %bitcast.46), calls=%async_computation | async-start | bytes 4194304 | tf_op jit(solution)/shard_map/all_to_all | solution.py:31
  10.7 0.0 copy-done.4
  10.7 2.0 convolution_convert_fusion.3
  12.7 44.4 %all-to-all-done = bf16[16,4,8,2048]{3,2,1,0:T(8,128)(2,1)S(1)} async-done(((bf16[16,4,8,2048]{3,2,1,0:T(8,128)(2,1)}), bf16[16,4,8,2048]{3,2,1,0:T(8,128)(2,1)S(1)}, u32[]{:S(2)}, u32[]{:S(2)}) %all-to-all-start) | async-done | bytes 2097184 | tf_op jit(solution)/shard_map/all_to_all | solution.py:31
  57.1 5.9 %all-to-all-start.1 = ((bf16[16,4,8,2048]{3,2,1,0:T(8,128)(2,1)}), bf16[16,4,8,2048]{3,2,1,0:T(8,128)(2,1)}, u32[]{:S(2)}, u32[]{:S(2)}) async-start(bf16[16,4,8,2048]{3,2,1,0:T(8,128)(2,1)} %bitcast.45), calls=%async_computation.1 | async-start | bytes 4194304 | tf_op jit(solution)/shard_map/all_to_all | solution.py:30
  63.0 9.4 %fusion.37 = f32[4,128,1024]{2,1,0:T(8,128)} fusion(bf16[4,2048,1024]{2,1,0:T(8,128)(2,1)} %param.15, bf16[16,4,8,2048]{3,2,1,0:T(8,128)(2,1)S(1)} %all-to-all-done), kind=kOutput, calls=%fused_computation.57 | convolution fusion | flops 2147483648 | bytes 20971520 | tf_op jit(solution)/shard_map/erd,edf->erf/dot_general | solution.py:41
  72.4 37.1 %all-to-all-done.1 = bf16[16,4,8,2048]{3,2,1,0:T(8,128)(2,1)} async-done(((bf16[16,4,8,2048]{3,2,1,0:T(8,128)(2,1)}), bf16[16,4,8,2048]{3,2,1,0:T(8,128)(2,1)}, u32[]{:S(2)}, u32[]{:S(2)}) %all-to-all-start.1) | async-done | bytes 2097184 | tf_op jit(solution)/shard_map/all_to_all | solution.py:30
  109.6 0.0 copy-start.2
  109.6 8.9 %fusion.38 = f32[4,128,1024]{2,1,0:T(8,128)S(1)} fusion(bf16[4,2048,1024]{2,1,0:T(8,128)(2,1)} %param.13, bf16[16,4,8,2048]{3,2,1,0:T(8,128)(2,1)} %all-to-all-done.1), kind=kOutput, calls=%fused_computation.58 | convolution fusion | flops 2147483648 | bytes 20971520 | tf_op jit(solution)/shard_map/erd,edf->erf/dot_general | solution.py:39
  118.5 0.0 copy-done.2
  118.5 11.7 %multiply_convert_fusion = (bf16[4,128,1024]{2,1,0:T(8,128)(2,1)}, bf16[4,128,1024]{2,1,0:T(8,128)(2,1)S(1)}, bf16[4,128,1024]{2,1,0:T(8,128)(2,1)}) fusion(f32[4,128,1024]{2,1,0:T(8,128)S(1)} %fusion.38, f32[4,128,1024]{2,1,0:T(8,128)S(1)} %copy-done.2, bf16[4,2048,1024]{2,1,0:T(8,128)(2,1)} %param.14, bf16[16,4,8,2048]{3,2,1,0:T(8,128)(2,1)} %all-to-all-done.1), kind=kOutput, calls=%fused_computation.24 | convolution fusion | flops 2155347968 | bytes 26214400 | tf_op jit(solution)/shard_map/erd,edf->erf/dot_general | solution.py:40
  130.2 13.4 %fusion.41 = f32[4,128,2048]{2,1,0:T(8,128)} fusion(bf16[4,128,1024]{2,1,0:T(8,128)(2,1)S(1)} %get-tuple-element.7, bf16[4,2048,1024]{2,1,0:T(8,128)(2,1)} %param.13), kind=kOutput, calls=%fused_computation.61 | convolution fusion | flops 2147483648 | bytes 22020096 | tf_op jit(solution)/shard_map/erf,edf->erd/dot_general | solution.py:50
  143.6 10.2 %fusion = bf16[4,16,8,2048]{3,2,1,0:T(8,128)(2,1)S(1)} fusion(f32[4,128,2048]{2,1,0:T(8,128)} %fusion.41, bf16[4,128,1024]{2,1,0:T(8,128)(2,1)} %get-tuple-element.8, bf16[4,2048,1024]{2,1,0:T(8,128)(2,1)} %param.14), kind=kOutput, calls=%fused_computation.6 | convolution fusion | flops 2149580800 | bytes 24117248 | tf_op jit(solution)/shard_map/erf,edf->erd/dot_general | solution.py:51
  153.8 1.6 copy.34
  155.4 5.9 %all-to-all-start.2 = ((bf16[16,4,8,2048]{3,2,1,0:T(8,128)(2,1)}), bf16[16,4,8,2048]{3,2,1,0:T(8,128)(2,1)}, u32[]{:S(2)}, u32[]{:S(2)}) async-start(bf16[16,4,8,2048]{3,2,1,0:T(8,128)(2,1)} %bitcast.44), calls=%async_computation.2 | async-start | bytes 4194304 | tf_op jit(solution)/shard_map/all_to_all | solution.py:53
  161.3 1.3 collective-permute-start.1
  162.5 0.2 collective-permute-start.2
  162.7 1.7 copy_bitcast_fusion.1
  164.5 0.2 constant_dynamic-slice_fusion.3
  164.7 1.3 collective-permute-start
  166.0 0.1 copy_bitcast_fusion.2
  166.1 0.0 copy-start.5
  166.1 0.0 copy-start.3
  166.2 0.2 constant_dynamic-slice_fusion.1
  166.3 0.3 collective-permute-start.3
  166.6 0.7 copy-done.5
  167.4 0.5 collective-permute-start.4
  167.9 62.7 %collective-permute-done = bf16[4,128,1024]{2,1,0:T(8,128)(2,1)S(1)} collective-permute-done((bf16[4,128,1024]{2,1,0:T(8,128)(2,1)S(1)}, bf16[4,128,1024]{2,1,0:T(8,128)(2,1)S(1)}, u32[]{:S(2)}, u32[]{:S(2)}) %collective-permute-start) | collective-permute-done | bytes 1048608 | tf_op jit(solution)/shard_map/ppermute | solution.py:35
  230.6 0.0 collective-permute-done.2
  230.6 0.0 copy-done.3
  230.6 4.7 %convolution_convert_fusion.1 = bf16[4,1024,1024]{2,1,0:T(8,128)(2,1)} fusion(bf16[4,128,1024]{2,1,0:T(8,128)(2,1)S(1)} %collective-permute-done.2, bf16[4,128,1024]{2,1,0:T(8,128)(2,1)S(1)} %copy-done.3, bf16[4,128,1024]{2,1,0:T(8,128)(2,1)S(1)} %collective-permute-done, bf16[4,128,1024]{2,1,0:T(8,128)(2,1)S(1)} %get-tuple-element.11), kind=kOutput, calls=%fused_computation.1 | convolution fusion | flops 2160066560 | bytes 12582912 | tf_op jit(solution)/shard_map/erd,erf->edf/dot_general | solution.py:60
  235.3 0.0 collective-permute-done.1
  235.3 4.7 %convolution_convert_fusion.2 = bf16[4,1024,1024]{2,1,0:T(8,128)(2,1)} fusion(bf16[4,128,1024]{2,1,0:T(8,128)(2,1)S(1)} %collective-permute-done.1, bf16[4,128,1024]{2,1,0:T(8,128)(2,1)S(1)} %get-tuple-element.7, bf16[4,128,1024]{2,1,0:T(8,128)(2,1)S(1)} %collective-permute-done, bf16[4,128,1024]{2,1,0:T(8,128)(2,1)S(1)} %get-tuple-element.11), kind=kOutput, calls=%fused_computation.2 | convolution fusion | flops 2160066560 | bytes 12582912 | tf_op jit(solution)/shard_map/erd,erf->edf/dot_general | solution.py:60
  240.0 13.0 %collective-permute-done.3 = bf16[4,128,1024]{2,1,0:T(8,128)(2,1)S(1)} collective-permute-done((bf16[4,128,1024]{2,1,0:T(8,128)(2,1)S(1)}, bf16[4,128,1024]{2,1,0:T(8,128)(2,1)S(1)}, u32[]{:S(2)}, u32[]{:S(2)}) %collective-permute-start.3) | collective-permute-done | bytes 1048608 | tf_op jit(solution)/shard_map/ppermute | solution.py:36
  253.1 22.5 %collective-permute-done.4 = bf16[4,128,1024]{2,1,0:T(8,128)(2,1)S(1)} collective-permute-done((bf16[4,128,1024]{2,1,0:T(8,128)(2,1)S(1)}, bf16[4,128,1024]{2,1,0:T(8,128)(2,1)S(1)}, u32[]{:S(2)}, u32[]{:S(2)}) %collective-permute-start.4) | collective-permute-done | bytes 1048608 | tf_op jit(solution)/shard_map/ppermute | solution.py:47
  275.5 0.0 copy-start.1
  275.5 4.7 %convolution_convert_fusion = bf16[4,1024,1024]{2,1,0:T(8,128)(2,1)} fusion(bf16[4,128,1024]{2,1,0:T(8,128)(2,1)S(1)} %collective-permute-done.3, bf16[4,128,1024]{2,1,0:T(8,128)(2,1)S(1)} %get-tuple-element.9, bf16[4,128,1024]{2,1,0:T(8,128)(2,1)S(1)} %collective-permute-done.4, bf16[4,128,1024]{2,1,0:T(8,128)(2,1)S(1)} %copy-done.5), kind=kOutput, calls=%fused_computation | convolution fusion | flops 2160066560 | bytes 12582912 | tf_op jit(solution)/shard_map/erd,erf->edf/dot_general | solution.py:60
  280.2 0.0 all-to-all-done.2
  280.2 3.3 %convolution_convert_fusion.5 = bf16[256,2048]{1,0:T(8,128)(2,1)} fusion(bf16[512,2048]{1,0:T(8,128)(2,1)} %bitcast.10, s32[256]{0:T(256)S(1)} %bitcast.52, s32[256]{0:T(256)S(1)} %bitcast.49), kind=kOutput, calls=%fused_computation.7 | convolution fusion | flops 538443776 | bytes 3147776 | tf_op jit(solution)/shard_map/pt,pd->td/dot_general | solution.py:55
  283.6 0.0 copy-done.1
  (1 shorter events, 0.0 us)
Async XLA Ops:
  0.6 1.5 copy-start
  4.2 6.5 %copy-start.4 = (bf16[256,2048]{1,0:T(8,128)(2,1)S(1)}, bf16[256,2048]{1,0:T(8,128)(2,1)}, u32[]{:S(2)}) copy-start(bf16[256,2048]{1,0:T(8,128)(2,1)} %param.8) | copy-start | bytes 3145732
  4.2 52.9 %all-to-all-start = ((bf16[16,4,8,2048]{3,2,1,0:T(8,128)(2,1)}), bf16[16,4,8,2048]{3,2,1,0:T(8,128)(2,1)S(1)}, u32[]{:S(2)}, u32[]{:S(2)}) async-start(bf16[16,4,8,2048]{3,2,1,0:T(8,128)(2,1)} %bitcast.46), calls=%async_computation | async-start | bytes 4194304 | tf_op jit(solution)/shard_map/all_to_all | solution.py:31
  57.1 52.4 %all-to-all-start.1 = ((bf16[16,4,8,2048]{3,2,1,0:T(8,128)(2,1)}), bf16[16,4,8,2048]{3,2,1,0:T(8,128)(2,1)}, u32[]{:S(2)}, u32[]{:S(2)}) async-start(bf16[16,4,8,2048]{3,2,1,0:T(8,128)(2,1)} %bitcast.45), calls=%async_computation.1 | async-start | bytes 4194304 | tf_op jit(solution)/shard_map/all_to_all | solution.py:30
  109.6 8.9 %copy-start.2 = (f32[4,128,1024]{2,1,0:T(8,128)S(1)}, f32[4,128,1024]{2,1,0:T(8,128)}, u32[]{:S(2)}) copy-start(f32[4,128,1024]{2,1,0:T(8,128)} %fusion.37) | copy-start | bytes 6291460
  155.4 124.8 %all-to-all-start.2 = ((bf16[16,4,8,2048]{3,2,1,0:T(8,128)(2,1)}), bf16[16,4,8,2048]{3,2,1,0:T(8,128)(2,1)}, u32[]{:S(2)}, u32[]{:S(2)}) async-start(bf16[16,4,8,2048]{3,2,1,0:T(8,128)(2,1)} %bitcast.44), calls=%async_computation.2 | async-start | bytes 4194304 | tf_op jit(solution)/shard_map/all_to_all | solution.py:53
  161.3 74.0 %collective-permute-start.1 = (bf16[4,128,1024]{2,1,0:T(8,128)(2,1)S(1)}, bf16[4,128,1024]{2,1,0:T(8,128)(2,1)S(1)}, u32[]{:S(2)}, u32[]{:S(2)}) collective-permute-start(bf16[4,128,1024]{2,1,0:T(8,128)(2,1)S(1)} %get-tuple-element.7), channel_id=1, source_target_pairs={{0,16},{16,0},{1,17},{17,1},{2,18},{18,2},{3,19},{19,3},{4,20},{20... | collective-permute-start | bytes 3145736 | tf_op jit(solution)/shard_map/ppermute | solution.py:48
  162.5 68.1 %collective-permute-start.2 = (bf16[4,128,1024]{2,1,0:T(8,128)(2,1)}, bf16[4,128,1024]{2,1,0:T(8,128)(2,1)S(1)}, u32[]{:S(2)}, u32[]{:S(2)}) collective-permute-start(bf16[4,128,1024]{2,1,0:T(8,128)(2,1)} %get-tuple-element.8), channel_id=1, source_target_pairs={{0,16},{16,0},{1,17},{17,1},{2,18},{18,2},{3,19},{19,3},{4,20},{20... | collective-permute-start | bytes 3145736 | tf_op jit(solution)/shard_map/ppermute | solution.py:49
  164.7 65.9 %collective-permute-start = (bf16[4,128,1024]{2,1,0:T(8,128)(2,1)S(1)}, bf16[4,128,1024]{2,1,0:T(8,128)(2,1)S(1)}, u32[]{:S(2)}, u32[]{:S(2)}) collective-permute-start(bf16[4,128,1024]{2,1,0:T(8,128)(2,1)S(1)} %get-tuple-element.12), channel_id=1, source_target_pairs={{0,16},{16,0},{1,17},{17,1},{2,18},{18,2},{3,19},{19,3},{4,20},{20... | collective-permute-start | bytes 3145736 | tf_op jit(solution)/shard_map/ppermute | solution.py:35
  166.1 1.2 copy-start.5
  166.1 64.4 %copy-start.3 = (bf16[4,128,1024]{2,1,0:T(8,128)(2,1)S(1)}, bf16[4,128,1024]{2,1,0:T(8,128)(2,1)}, u32[]{:S(2)}) copy-start(bf16[4,128,1024]{2,1,0:T(8,128)(2,1)} %get-tuple-element.8) | copy-start | bytes 3145732
  166.3 86.7 %collective-permute-start.3 = (bf16[4,128,1024]{2,1,0:T(8,128)(2,1)S(1)}, bf16[4,128,1024]{2,1,0:T(8,128)(2,1)S(1)}, u32[]{:S(2)}, u32[]{:S(2)}) collective-permute-start(bf16[4,128,1024]{2,1,0:T(8,128)(2,1)S(1)} %get-tuple-element.10), channel_id=1, source_target_pairs={{0,16},{16,0},{1,17},{17,1},{2,18},{18,2},{3,19},{19,3},{4,20},{20... | collective-permute-start | bytes 3145736 | tf_op jit(solution)/shard_map/ppermute | solution.py:36
  167.4 108.2 %collective-permute-start.4 = (bf16[4,128,1024]{2,1,0:T(8,128)(2,1)S(1)}, bf16[4,128,1024]{2,1,0:T(8,128)(2,1)S(1)}, u32[]{:S(2)}, u32[]{:S(2)}) collective-permute-start(bf16[4,128,1024]{2,1,0:T(8,128)(2,1)S(1)} %copy-done.5), channel_id=1, source_target_pairs={{0,16},{16,0},{1,17},{17,1},{2,18},{18,2},{3,19},{19,3},{4,20},{20... | collective-permute-start | bytes 3145736 | tf_op jit(solution)/shard_map/ppermute | solution.py:47
  275.5 8.0 %copy-start.1 = (bf16[256,2048]{1,0:T(8,128)(2,1)S(1)}, bf16[256,2048]{1,0:T(8,128)(2,1)}, u32[]{:S(2)}) copy-start(bf16[256,2048]{1,0:T(8,128)(2,1)} %param.9) | copy-start | bytes 3145732

commit v2 on v1

v2 whole, which is shorter than its diff:
```python
import functools

import jax
import jax.numpy as jnp
from jax import lax
from jax.experimental import pallas as pl
from jax.experimental.pallas import tpu as pltpu
from jax.sharding import PartitionSpec as P

E = 64
BF = jnp.bfloat16
F32 = jnp.float32
MESH = pl.DeviceIdType.MESH
NT = (((1,), (1,)), ((), ()))


def expert_kernel(
    dims, pos, wts, tok, gro, wg, wu, wd,
    ret, xs, gs, acts, ggs, ugs,
    send, recv, wbuf, xg, hid, back,
    send_sem, recv_sem, w_sem, back_sem, ret_sem, near_sem, far_send, far_recv,
):
    group, nexp, el, slots, width, ff, nbuf = dims
    half = width // 2
    rows = group * slots
    tile = min(128, rows)
    per = tile // slots
    blocks = rows // tile
    fstep = min(ff, 256)
    dstep = min(width, 512)
    me_dp = lax.axis_index("dp")
    other = 1 - me_dp
    me = lax.axis_index("seq") * nexp + lax.axis_index("expert")

    def at(j):
        return {"seq": lax.div(j, nexp), "expert": lax.rem(j, nexp)}

    def weights(e, slot):
        return [
            pltpu.make_async_copy(w.at[e], wbuf.at[slot, i], w_sem.at[slot, i])
            for i, w in enumerate((wg, wu, wd))
        ]

    for e in range(nbuf):
        for c in weights(e, e):
            c.start()

    barrier = pltpu.get_barrier_semaphore()

    @pl.loop(1, group)
    def _(k):
        j = lax.rem(me + k, group)
        pl.semaphore_signal(barrier, inc=1, device_id=at(j), device_id_type=MESH)

    pl.semaphore_signal(barrier, inc=1, device_id={"dp": other}, device_id_type=MESH)
    pl.semaphore_wait(barrier, group)

    @pl.loop(0, el)
    def _(e):
        @pl.loop(0, blocks)
        def _(b):
            r = lax.broadcasted_iota(jnp.int32, (tile, pos.shape[1]), 0)
            place = ((b * per + lax.div(r, slots)) * el + e) * slots + lax.rem(r, slots)
            hit0 = pos[0:1, :] == place
            hit1 = pos[1:2, :] == place
            pick = (jnp.where(hit0, 1.0, 0.0) + jnp.where(hit1, 1.0, 0.0)).astype(BF)
            weigh = (jnp.where(hit0, wts[0:1, :], 0.0) + jnp.where(hit1, wts[1:2, :], 0.0)).astype(BF)

            @pl.loop(0, width // dstep)
            def _(d):
                cols = pl.ds(pl.multiple_of(d * dstep, dstep), dstep)
                devs = pl.ds(b * per, per)
                px = jnp.dot(pick, tok[:, cols], preferred_element_type=F32)
                send[e, devs, 0, :, cols] = px.reshape(per, slots, dstep).astype(BF)
                pg = jnp.dot(weigh, gro[:, cols], preferred_element_type=F32)
                send[e, devs, 1, :, cols] = pg.reshape(per, slots, dstep).astype(BF)

        pltpu.make_async_copy(send.at[e, me], recv.at[e, me], recv_sem.at[e]).start()

        @pl.loop(1, group)
        def _(k):
            j = lax.rem(me + k, group)
            pltpu.make_async_remote_copy(
                src_ref=send.at[e, j], dst_ref=recv.at[e, me],
                send_sem=send_sem.at[e], recv_sem=recv_sem.at[e],
                device_id=at(j), device_id_type=MESH,
            ).start()

    def swaps(e):
        near = pl.ds(pl.multiple_of(me_dp * half, 128), half)
        away = pl.ds(pl.multiple_of(other * half, 128), half)
        pairs = [
            (xg.at[e, 0, :, near], xg.at[e, 0, :, away], xs),
            (xg.at[e, 1, :, near], xg.at[e, 1, :, away], gs),
        ] + [(hid.at[e, i], hid.at[e, i], o) for i, o in enumerate((acts, ggs, ugs))]
        out = []
        for i, (own, sent, o) in enumerate(pairs):
            local = pltpu.make_async_copy(own, o.at[e, 0], near_sem.at[e, i])
            remote = pltpu.make_async_remote_copy(
                src_ref=sent, dst_ref=o.at[e, 1],
                send_sem=far_send.at[e, i], recv_sem=far_recv.at[e, i],
                device_id={"dp": other}, device_id_type=MESH,
            )
            out.append((local, remote))
        return out

    @pl.loop(0, el)
    def _(e):
        slot = lax.rem(e, nbuf)
        pltpu.make_async_copy(recv.at[e], recv.at[e], recv_sem.at[e]).wait()

        @pl.loop(0, blocks)
        def _(b):
            @pl.loop(0, width // dstep)
            def _(d):
                cols = pl.ds(pl.multiple_of(d * dstep, dstep), dstep)
                for i in range(2):
                    v = recv[e, pl.ds(b * per, per), i, :, cols].astype(F32)
                    xg[e, i, pl.ds(pl.multiple_of(b * tile, tile), tile), cols] = v.reshape(tile, dstep).astype(BF)

        pairs = swaps(e)
        for local, remote in pairs[:2]:
            local.start()
            remote.start()
        for c in weights(e, slot):
            c.wait()

        @pl.loop(0, ff // fstep)
        def _(f):
            cols = pl.ds(pl.multiple_of(f * fstep, fstep), fstep)

            @pl.loop(0, blocks)
            def _(b):
                rs = pl.ds(pl.multiple_of(b * tile, tile), tile)
                x = xg[e, 0, rs, :]
                gp = jnp.dot(x, wbuf[slot, 0, :, cols], preferred_element_type=F32)
                up = jnp.dot(x, wbuf[slot, 1, :, cols], preferred_element_type=F32)
                ag = jnp.dot(xg[e, 1, rs, :], wbuf[slot, 2, :, cols], preferred_element_type=F32)
                sig = jax.nn.sigmoid(gp)
                silu = gp * sig
                hid[e, 0, rs, cols] = (silu * up).astype(BF)
                hid[e, 1, rs, cols] = (ag * up * sig * (1.0 + gp * (1.0 - sig))).astype(BF)
                hid[e, 2, rs, cols] = (ag * silu).astype(BF)

        for local, remote in pairs[2:]:
            local.start()
            remote.start()

        @pl.loop(0, width // dstep)
        def _(d):
            cols = pl.ds(pl.multiple_of(d * dstep, dstep), dstep)

            @pl.loop(0, blocks)
            def _(b):
                rs = pl.ds(pl.multiple_of(b * tile, tile), tile)
                t = lax.dot_general(hid[e, 1, rs, :], wbuf[slot, 0, cols, :], NT, preferred_element_type=F32)
                t = t + lax.dot_general(hid[e, 2, rs, :], wbuf[slot, 1, cols, :], NT, preferred_element_type=F32)
                back[e, pl.ds(b * per, per), :, cols] = t.reshape(per, slots, dstep).astype(BF)

        pltpu.make_async_copy(back.at[e, me], ret.at[me, e], ret_sem).start()

        @pl.loop(1, group)
        def _(k):
            j = lax.rem(me + k, group)
            pltpu.make_async_remote_copy(
                src_ref=back.at[e, j], dst_ref=ret.at[me, e],
                send_sem=back_sem.at[e], recv_sem=ret_sem,
                device_id=at(j), device_id_type=MESH,
            ).start()

        @pl.when(e + nbuf < el)
        def _():
            for c in weights(e + nbuf, slot):
                c.start()

    @pl.loop(0, el)
    def _(e):
        for local, remote in swaps(e):
            local.wait()
            remote.wait()
        rest = pl.ds(0, group - 1)
        pltpu.make_async_copy(send.at[e, rest], send.at[e, rest], send_sem.at[e]).wait()
        pltpu.make_async_copy(back.at[e, rest], back.at[e, rest], back_sem.at[e]).wait()

    pltpu.make_async_copy(ret, ret, ret_sem).wait()


def per_device(tokens, grad_out, route_weights, expert_ids, route_slots, w_gate, w_up, w_down):
    nexp = lax.axis_size("expert")
    group = lax.axis_size("seq") * nexp
    el, width, ff = w_gate.shape
    cells = tokens.shape[0]
    slots = 2 * cells // E
    half = width // 2
    rows = group * slots
    nbuf = min(2, el)
    position = expert_ids * slots + route_slots
    dims = (group, nexp, el, slots, width, ff, nbuf)
    vmem = pl.BlockSpec(memory_space=pltpu.VMEM)
    hbm = pl.BlockSpec(memory_space=pl.ANY)
    dma = pltpu.SemaphoreType.DMA
    ret, xs, gs, acts, ggs, ugs = pl.pallas_call(
        functools.partial(expert_kernel, dims),
        out_shape=[
            jax.ShapeDtypeStruct((group, el, slots, width), BF),
            jax.ShapeDtypeStruct((el, 2, rows, half), BF),
            jax.ShapeDtypeStruct((el, 2, rows, half), BF),
            jax.ShapeDtypeStruct((el, 2, rows, ff), BF),
            jax.ShapeDtypeStruct((el, 2, rows, ff), BF),
            jax.ShapeDtypeStruct((el, 2, rows, ff), BF),
        ],
        in_specs=[vmem] * 4 + [hbm] * 3,
        out_specs=[hbm] * 6,
        scratch_shapes=[
            pltpu.VMEM((el, group, 2, slots, width), BF),
            pltpu.VMEM((el, group, 2, slots, width), BF),
            pltpu.VMEM((nbuf, 3, width, ff), BF),
            pltpu.VMEM((el, 2, rows, width), BF),
            pltpu.VMEM((el, 3, rows, ff), BF),
            pltpu.VMEM((el, group, slots, width), BF),
            dma((el,)),
            dma((el,)),
            dma((nbuf, 3)),
            dma((el,)),
            dma,
            dma((el, 5)),
            dma((el, 5)),
            dma((el, 5)),
        ],
        compiler_params=pltpu.CompilerParams(
            collective_id=0, has_side_effects=True, vmem_limit_bytes=58 * 1024 * 1024
        ),
    )(position.T, route_weights.astype(F32).T, tokens, grad_out, w_gate, w_up, w_down)

    place = jnp.arange(E * slots, dtype=jnp.int32)[None, :]
    take = (position[:, 0:1] == place).astype(BF) + (position[:, 1:2] == place).astype(BF)
    ret = ret.reshape(E * slots, width)
    grad_tokens = jnp.dot(take, ret, preferred_element_type=F32).astype(BF)

    def wgrad(a, b):
        a = a.reshape(el, 2 * rows, half)
        b = b.reshape(el, 2 * rows, ff)
        return jnp.einsum("erd,erf->edf", a, b, preferred_element_type=F32).astype(BF)

    return grad_tokens, wgrad(xs, ggs), wgrad(xs, ugs), wgrad(gs, acts)


def solution(mesh):
    cell = P(("dp", "seq", "expert"), None)
    held = P(("seq", "expert"), None, None)
    grad = P(("seq", "expert"), "dp", None)
    return jax.shard_map(
        per_device,
        mesh=mesh,
        in_specs=(cell,) * 5 + (held,) * 3,
        out_specs=(cell, grad, grad, grad),
        check_vma=False,
    )
```

time: 286 us -> 188 us (0.66)
  waiting for transfers between devices: 180 us -> 0 us
  Pallas kernels: 0 us -> 162 us
  matrix products: 75.2 us -> 22.7 us
  starting transfers between devices: 21.8 us -> 0 us
  local copies, waits for them, and re-layouts: 5.43 us -> 0.02 us
    pallas_call x0 -> x1, Pallas kernels: none -> 162 us  [per_device(): pl.pallas_call(functools.partial(expert_kernel, dims), out_shape=[jax.Sha...]
    ppermute x5 -> x0, waiting for transfers between devices: 98.2 us -> none  [the longest x1 62.7 us: per_device(): lax.ppermute(lax.dynamic_slice_in_dim(x, (1 - dp) * half, half, 2), 'dp',...]
    all_to_all x3 -> x0, waiting for transfers between devices: 81.5 us -> none  [the longest x1 44.4 us: per_device(): g = lax.all_to_all(send_g, axes, split_axis=0, concat_axis=0, tiled=True)]
    dot_general x8 -> x1, matrix products: 61 us -> 3.51 us  [per_device(): grad_tokens = jnp.dot(take, ret, preferred_element_type=F32).astype(BF)]
    all_to_all x3 -> x0, starting transfers between devices: 18.2 us -> none  [the longest x1 6.46 us: per_device(): g = lax.all_to_all(send_g, axes, split_axis=0, concat_axis=0, tiled=True)]
    dot_general x3, matrix products: 14.1 us -> 19.2 us  [wgrad(): jnp.einsum('erd,erf->edf', a, b, preferred_element_type=F32).astype(BF)]
    ppermute x5 -> x0, starting transfers between devices: 3.58 us -> none  [the longest x1 1.31 us: per_device(): lax.ppermute(lax.dynamic_slice_in_dim(x, (1 - dp) * half, half, 2), 'dp',...]
    reshape x3 -> x0, local copies, waits for them, and re-layouts: 3.47 us -> none  [the longest x1 1.73 us: per_device(): x = x.transpose(1, 0, 2, 3).reshape(el, rows, width)]
  transfers between devices with their start and end apart: 8 -> 0, of which waited for: 5 -> 0; matrix products, arithmetic and copies ran while one was open for 10% -> 0% of each run, Pallas kernels for 0% -> 0%
where the time goes in v2:
time: 188 us
  Pallas kernels  162 us (86%)
  matrix products  22.7 us (12%)
  other arithmetic  1.96 us (1%)
    pallas_call x1, Pallas kernels, per_device(): pl.pallas_call(functools.partial(expert_kernel, dims), out_shape=[jax.Sha...  162 us
    dot_general x3, matrix products, wgrad(): jnp.einsum('erd,erf->edf', a, b, preferred_element_type=F32).astype(BF)  19.2 us

profile of v2, /device:TPU:29, one launch (start us, length us, event | category | flops | bytes accessed | tf_op | source)
XLA Modules:
  0.0 187.7 jit_solution(6856317286648373431)
XLA Ops:
  0.6 0.7 multiply_add_fusion
  1.3 0.0 copy-start.4
  1.3 1.3 convert_bitcast_fusion.wts
  2.6 0.0 copy-done.4
  2.6 162.4 %shard_map.111 = (bf16[16,4,8,2048]{3,2,1,0:T(8,128)(2,1)}, bf16[4,2,128,1024]{3,2,1,0:T(8,128)(2,1)}, bf16[4,2,128,1024]{3,2,1,0:T(8,128)(2,1)}, bf16[4,2,128,1...) custom-call(s32[2,256]{1,0:T(2,128)} %bitcast.24, ...), custom_call_target="tpu_custom_call" | custom-call | tf_op jit(solution)/shard_map/pallas_call | solution.py:202
  165.0 0.0 copy-start
  165.0 3.5 %convolution_convert_fusion.3 = bf16[256,2048]{1,0:T(8,128)(2,1)} fusion(bf16[512,2048]{1,0:T(8,128)(2,1)} %bitcast.27, s32[256]{0:T(256)S(1)} %bitcast.26, s32[256]{0:T(256)S(1)} %bitcast.25), kind=kOutput, calls=%fused_computation.3 | convolution fusion | flops 538443776 | bytes 3147776 | tf_op jit(solution)/shard_map/dot_general | solution.py:238
  168.5 0.0 copy-done
  168.5 0.0 copy-start.3
  168.5 7.5 %convolution_convert_fusion.1 = bf16[4,1024,1024]{2,1,0:T(8,128)(2,1)} fusion(bf16[4,256,1024]{2,1,0:T(8,128)(2,1)S(1)} %bitcast.18, bf16[4,256,1024]{2,1,0:T(8,128)(2,1)} %bitcast.23), kind=kOutput, calls=%fused_computation.1 | convolution fusion | flops 2151677952 | bytes 12582912 | tf_op jit(solution)/shard_map/erd,erf->edf/dot_general | solution.py:243
  176.1 0.0 copy-done.3
  176.1 0.0 copy-start.1
  176.1 0.0 copy-start.2
  176.1 5.8 %convolution_convert_fusion.2 = bf16[4,1024,1024]{2,1,0:T(8,128)(2,1)} fusion(bf16[4,256,1024]{2,1,0:T(8,128)(2,1)S(1)} %bitcast.19, bf16[4,256,1024]{2,1,0:T(8,128)(2,1)S(1)} %bitcast.22), kind=kOutput, calls=%fused_computation.2 | convolution fusion | flops 2151677952 | bytes 12582912 | tf_op jit(solution)/shard_map/erd,erf->edf/dot_general | solution.py:243
  181.9 0.0 copy-done.1
  181.9 0.0 copy-done.2
  181.9 5.8 %convolution_convert_fusion = bf16[4,1024,1024]{2,1,0:T(8,128)(2,1)} fusion(bf16[4,256,1024]{2,1,0:T(8,128)(2,1)S(1)} %bitcast.20, bf16[4,256,1024]{2,1,0:T(8,128)(2,1)S(1)} %bitcast.21), kind=kOutput, calls=%fused_computation | convolution fusion | flops 2151677952 | bytes 12582912 | tf_op jit(solution)/shard_map/erd,erf->edf/dot_general | solution.py:243
  (1 shorter events, 0.0 us)
Async XLA Ops:
  1.3 1.3 copy-start.4
  165.0 3.5 %copy-start = (bf16[4,2,128,1024]{3,2,1,0:T(8,128)(2,1)S(1)}, bf16[4,2,128,1024]{3,2,1,0:T(8,128)(2,1)}, u32[]{:S(2)}) copy-start(bf16[4,2,128,1024]{3,2,1,0:T(8,128)(2,1)} %get-tuple-element.11) | copy-start | bytes 6291460
  168.5 7.5 %copy-start.3 = (bf16[4,2,128,1024]{3,2,1,0:T(8,128)(2,1)S(1)}, bf16[4,2,128,1024]{3,2,1,0:T(8,128)(2,1)}, u32[]{:S(2)}) copy-start(bf16[4,2,128,1024]{3,2,1,0:T(8,128)(2,1)} %get-tuple-element.12) | copy-start | bytes 6291460
  176.1 5.8 %copy-start.1 = (bf16[4,2,128,1024]{3,2,1,0:T(8,128)(2,1)S(1)}, bf16[4,2,128,1024]{3,2,1,0:T(8,128)(2,1)}, u32[]{:S(2)}) copy-start(bf16[4,2,128,1024]{3,2,1,0:T(8,128)(2,1)} %get-tuple-element.14) | copy-start | bytes 6291460
  176.1 5.8 %copy-start.2 = (bf16[4,2,128,1024]{3,2,1,0:T(8,128)(2,1)S(1)}, bf16[4,2,128,1024]{3,2,1,0:T(8,128)(2,1)}, u32[]{:S(2)}) copy-start(bf16[4,2,128,1024]{3,2,1,0:T(8,128)(2,1)} %get-tuple-element.15) | copy-start | bytes 6291460

commit v3 on v2

v3 whole, which is shorter than its diff:
```python
import functools

import jax
import jax.numpy as jnp
from jax import lax
from jax.experimental import pallas as pl
from jax.experimental.pallas import tpu as pltpu
from jax.sharding import PartitionSpec as P

E = 64
BF = jnp.bfloat16
F32 = jnp.float32
MESH = pl.DeviceIdType.MESH
NT = (((1,), (1,)), ((), ()))


def expert_kernel(
    dims, pos, wts, tok, gro, wg, wu, wd,
    ret, xs, gs, acts, ggs, ugs,
    send, recv, far, wbuf, xg, hid, back,
    send_sem, recv_sem, w_sem, back_sem, ret_sem, keep_sem, far_send, far_recv,
):
    group, nexp, el, slots, width, ff, nbuf = dims
    half = width // 2
    rows = group * slots
    tile = min(128, rows)
    per = tile // slots
    blocks = rows // tile
    fstep = min(ff, 256)
    dstep = min(width, 512)
    me_dp = lax.axis_index("dp")
    other = 1 - me_dp
    me = lax.axis_index("seq") * nexp + lax.axis_index("expert")

    def at(j):
        return {"seq": lax.div(j, nexp), "expert": lax.rem(j, nexp)}

    def weights(e, slot):
        return [
            pltpu.make_async_copy(w.at[e], wbuf.at[slot, i], w_sem.at[slot, i])
            for i, w in enumerate((wg, wu, wd))
        ]

    for c in weights(0, 0):
        c.start()

    barrier = pltpu.get_barrier_semaphore()

    @pl.loop(1, group)
    def _(k):
        j = lax.rem(me + k, group)
        pl.semaphore_signal(barrier, inc=1, device_id=at(j), device_id_type=MESH)

    pl.semaphore_signal(barrier, inc=1, device_id={"dp": other}, device_id_type=MESH)
    pl.semaphore_wait(barrier, group)

    @pl.loop(0, el)
    def _(e):
        @pl.loop(0, blocks)
        def _(b):
            r = lax.broadcasted_iota(jnp.int32, (tile, pos.shape[1]), 0)
            place = ((b * per + lax.div(r, slots)) * el + e) * slots + lax.rem(r, slots)
            hit0 = pos[0:1, :] == place
            hit1 = pos[1:2, :] == place
            pick = (jnp.where(hit0, 1.0, 0.0) + jnp.where(hit1, 1.0, 0.0)).astype(BF)
            weigh = (jnp.where(hit0, wts[0:1, :], 0.0) + jnp.where(hit1, wts[1:2, :], 0.0)).astype(BF)

            @pl.loop(0, width // dstep)
            def _(d):
                cols = pl.ds(pl.multiple_of(d * dstep, dstep), dstep)
                devs = pl.ds(b * per, per)
                px = jnp.dot(pick, tok[:, cols], preferred_element_type=F32)
                send[e, devs, 0, :, cols] = px.reshape(per, slots, dstep).astype(BF)
                pg = jnp.dot(weigh, gro[:, cols], preferred_element_type=F32)
                send[e, devs, 1, :, cols] = pg.reshape(per, slots, dstep).astype(BF)

        pltpu.make_async_copy(send.at[e, me], recv.at[e, me], recv_sem.at[e]).start()

        @pl.loop(1, group)
        def _(k):
            j = lax.rem(me + k, group)
            pltpu.make_async_remote_copy(
                src_ref=send.at[e, j], dst_ref=recv.at[e, me],
                send_sem=send_sem.at[e], recv_sem=recv_sem.at[e],
                device_id=at(j), device_id_type=MESH,
            ).start()

    def swap(e):
        return pltpu.make_async_remote_copy(
            src_ref=recv.at[e], dst_ref=far.at[e],
            send_sem=far_send.at[e], recv_sem=far_recv.at[e],
            device_id={"dp": other}, device_id_type=MESH,
        )

    def keep(e, slot, part):
        cols = pl.ds(pl.multiple_of(me_dp * half, 128), half)
        pairs = [(xg.at[slot, part, 0, :, cols], xs), (xg.at[slot, part, 1, :, cols], gs)]
        pairs += [(hid.at[slot, part, i], o) for i, o in enumerate((acts, ggs, ugs))]
        return [
            pltpu.make_async_copy(src, o.at[e, part], keep_sem.at[slot, part, i])
            for i, (src, o) in enumerate(pairs)
        ]

    def forward(e, slot, part, got):
        @pl.when(e >= nbuf)
        def _():
            for c in keep(e - nbuf, slot, part):
                c.wait()

        @pl.loop(0, blocks)
        def _(b):
            rs = pl.ds(pl.multiple_of(b * tile, tile), tile)

            @pl.loop(0, width // dstep)
            def _(d):
                cols = pl.ds(pl.multiple_of(d * dstep, dstep), dstep)
                for i in range(2):
                    v = got[e, pl.ds(b * per, per), i, :, cols].astype(F32)
                    xg[slot, part, i, rs, cols] = v.reshape(tile, dstep).astype(BF)

        copies = keep(e, slot, part)
        for c in copies[:2]:
            c.start()
        if part == 0:
            for c in weights(e, slot):
                c.wait()

        @pl.loop(0, ff // fstep)
        def _(f):
            cols = pl.ds(pl.multiple_of(f * fstep, fstep), fstep)

            @pl.loop(0, blocks)
            def _(b):
                rs = pl.ds(pl.multiple_of(b * tile, tile), tile)
                x = xg[slot, part, 0, rs, :]
                gp = jnp.dot(x, wbuf[slot, 0, :, cols], preferred_element_type=F32)
                up = jnp.dot(x, wbuf[slot, 1, :, cols], preferred_element_type=F32)
                ag = jnp.dot(xg[slot, part, 1, rs, :], wbuf[slot, 2, :, cols], preferred_element_type=F32)
                sig = jax.nn.sigmoid(gp)
                silu = gp * sig
                hid[slot, part, 0, rs, cols] = (silu * up).astype(BF)
                hid[slot, part, 1, rs, cols] = (ag * up * sig * (1.0 + gp * (1.0 - sig))).astype(BF)
                hid[slot, part, 2, rs, cols] = (ag * silu).astype(BF)

        for c in copies[2:]:
            c.start()

    def peer_rows(e):
        swap(e).wait_recv()
        forward(e, lax.rem(e, nbuf), 1, far)

    @pl.loop(0, el)
    def _(e):
        slot = lax.rem(e, nbuf)
        pltpu.make_async_copy(recv.at[e], recv.at[e], recv_sem.at[e]).wait()
        swap(e).start()
        forward(e, slot, 0, recv)

        @pl.loop(0, width // dstep)
        def _(d):
            cols = pl.ds(pl.multiple_of(d * dstep, dstep), dstep)

            @pl.loop(0, blocks)
            def _(b):
                rs = pl.ds(pl.multiple_of(b * tile, tile), tile)
                t = lax.dot_general(hid[slot, 0, 1, rs, :], wbuf[slot, 0, cols, :], NT, preferred_element_type=F32)
                t = t + lax.dot_general(hid[slot, 0, 2, rs, :], wbuf[slot, 1, cols, :], NT, preferred_element_type=F32)
                back[e, pl.ds(b * per, per), :, cols] = t.reshape(per, slots, dstep).astype(BF)

        pltpu.make_async_copy(back.at[e, me], ret.at[me, e], ret_sem).start()

        @pl.loop(1, group)
        def _(k):
            j = lax.rem(me + k, group)
            pltpu.make_async_remote_copy(
                src_ref=back.at[e, j], dst_ref=ret.at[me, e],
                send_sem=back_sem.at[e], recv_sem=ret_sem,
                device_id=at(j), device_id_type=MESH,
            ).start()

        @pl.when(e > 0)
        def _():
            peer_rows(e - 1)

        @pl.when(e + 1 < el)
        def _():
            for c in weights(e + 1, lax.rem(e + 1, nbuf)):
                c.start()

    peer_rows(el - 1)
    for e in range(el - nbuf, el):
        for part in range(2):
            for c in keep(e, e % nbuf, part):
                c.wait()

    @pl.loop(0, el)
    def _(e):
        swap(e).wait_send()
        rest = pl.ds(0, group - 1)
        pltpu.make_async_copy(send.at[e, rest], send.at[e, rest], send_sem.at[e]).wait()
        pltpu.make_async_copy(back.at[e, rest], back.at[e, rest], back_sem.at[e]).wait()

    pltpu.make_async_copy(ret, ret, ret_sem).wait()


def grads_kernel(pos, ret, xs, gs, acts, ggs, ugs, gtok, ogate, oup, odown):
    place = lax.broadcasted_iota(jnp.int32, (pos.shape[0], ret.shape[0]), 1)
    take = jnp.where(pos[:, 0:1] == place, 1.0, 0.0) + jnp.where(pos[:, 1:2] == place, 1.0, 0.0)
    gtok[...] = jnp.dot(take.astype(BF), ret[...], preferred_element_type=F32).astype(BF)
    xt = xs[0].T
    ogate[0] = jnp.dot(xt, ggs[0], preferred_element_type=F32).astype(BF)
    oup[0] = jnp.dot(xt, ugs[0], preferred_element_type=F32).astype(BF)
    odown[0] = jnp.dot(gs[0].T, acts[0], preferred_element_type=F32).astype(BF)


def per_device(tokens, grad_out, route_weights, expert_ids, route_slots, w_gate, w_up, w_down):
    nexp = lax.axis_size("expert")
    group = lax.axis_size("seq") * nexp
    el, width, ff = w_gate.shape
    cells = tokens.shape[0]
    slots = 2 * cells // E
    half = width // 2
    rows = group * slots
    nbuf = min(2, el)
    position = expert_ids * slots + route_slots
    dims = (group, nexp, el, slots, width, ff, nbuf)
    vmem = pl.BlockSpec(memory_space=pltpu.VMEM)
    hbm = pl.BlockSpec(memory_space=pl.ANY)
    dma = pltpu.SemaphoreType.DMA
    ret, xs, gs, acts, ggs, ugs = pl.pallas_call(
        functools.partial(expert_kernel, dims),
        out_shape=[
            jax.ShapeDtypeStruct((group, el, slots, width), BF),
            jax.ShapeDtypeStruct((el, 2, rows, half), BF),
            jax.ShapeDtypeStruct((el, 2, rows, half), BF),
            jax.ShapeDtypeStruct((el, 2, rows, ff), BF),
            jax.ShapeDtypeStruct((el, 2, rows, ff), BF),
            jax.ShapeDtypeStruct((el, 2, rows, ff), BF),
        ],
        in_specs=[vmem] * 4 + [hbm] * 3,
        out_specs=[hbm] * 6,
        scratch_shapes=[
            pltpu.VMEM((el, group, 2, slots, width), BF),
            pltpu.VMEM((el, group, 2, slots, width), BF),
            pltpu.VMEM((el, group, 2, slots, width), BF),
            pltpu.VMEM((nbuf, 3, width, ff), BF),
            pltpu.VMEM((nbuf, 2, 2, rows, width), BF),
            pltpu.VMEM((nbuf, 2, 3, rows, ff), BF),
            pltpu.VMEM((el, group, slots, width), BF),
            dma((el,)),
            dma((el,)),
            dma((nbuf, 3)),
            dma((el,)),
            dma,
            dma((nbuf, 2, 5)),
            dma((el,)),
            dma((el,)),
        ],
        compiler_params=pltpu.CompilerParams(
            collective_id=0, has_side_effects=True, vmem_limit_bytes=58 * 1024 * 1024
        ),
    )(position.T, route_weights.astype(F32).T, tokens, grad_out, w_gate, w_up, w_down)

    cut = 2
    dcol = half // cut
    tcol = width // (el * cut)
    deep = 2 * rows
    flat = [v.reshape(el, deep, v.shape[-1]) for v in (xs, gs, acts, ggs, ugs)]
    grad = jax.ShapeDtypeStruct((el, half, ff), BF)
    lhs = pl.BlockSpec((1, deep, dcol), lambda e, d: (e, 0, d))
    rhs = pl.BlockSpec((1, deep, ff), lambda e, d: (e, 0, 0))
    out = pl.BlockSpec((1, dcol, ff), lambda e, d: (e, d, 0))
    return pl.pallas_call(
        grads_kernel,
        grid=(el, cut),
        out_shape=[jax.ShapeDtypeStruct((cells, width), BF), grad, grad, grad],
        in_specs=[
            pl.BlockSpec((cells, 2), lambda e, d: (0, 0)),
            pl.BlockSpec((E * slots, tcol), lambda e, d: (0, e * cut + d)),
            lhs, lhs, rhs, rhs, rhs,
        ],
        out_specs=[pl.BlockSpec((cells, tcol), lambda e, d: (0, e * cut + d)), out, out, out],
        compiler_params=pltpu.CompilerParams(vmem_limit_bytes=48 * 1024 * 1024),
    )(position, ret.reshape(E * slots, width), *flat)


def solution(mesh):
    cell = P(("dp", "seq", "expert"), None)
    held = P(("seq", "expert"), None, None)
    grad = P(("seq", "expert"), "dp", None)
    return jax.shard_map(
        per_device,
        mesh=mesh,
        in_specs=(cell,) * 5 + (held,) * 3,
        out_specs=(cell, grad, grad, grad),
        check_vma=False,
    )
```

time: 188 us -> 178 us (0.947)
  matrix products: 22.7 us -> 0 us
  Pallas kernels: 162 us -> 172 us
  local copies, waits for them, and re-layouts: 0.02 us -> 3.31 us
    dot_general x4 -> x0, matrix products: 22.7 us -> none  [the longest x3 19.2 us: wgrad(): jnp.einsum('erd,erf->edf', a, b, preferred_element_type=F32).astype(BF)]
    pallas_call x0 -> x1, Pallas kernels: none -> 17.3 us  [per_device(): pl.pallas_call(grads_kernel, grid=(el, cut), out_shape=[jax.ShapeDtypeStr...]
    pallas_call x1, Pallas kernels: 162 us -> 154 us  [per_device(): pl.pallas_call(functools.partial(expert_kernel, dims), out_shape=[jax.Sha...]
    unnamed x10 -> x6, local copies, waits for them, and re-layouts: 0.02 us -> 3.18 us
where the time goes in v3:
time: 178 us
  Pallas kernels  172 us (97%)
  local copies, waits for them, and re-layouts  3.31 us (2%)
  other arithmetic  1.96 us (1%)
    pallas_call x1, Pallas kernels, per_device(): pl.pallas_call(functools.partial(expert_kernel, dims), out_shape=[jax.Sha...  154 us
    pallas_call x1, Pallas kernels, per_device(): pl.pallas_call(grads_kernel, grid=(el, cut), out_shape=[jax.ShapeDtypeStr...  17.3 us

profile of v3, /device:TPU:29, one launch (start us, length us, event | category | flops | bytes accessed | tf_op | source)
XLA Modules:
  0.0 177.7 jit_solution(4190526547610663743)
XLA Ops:
  0.6 0.7 multiply_add_fusion
  1.3 0.0 copy-start.2
  1.3 1.3 convert_bitcast_fusion.wts
  2.6 0.1 copy.16.pos
  2.7 0.0 copy-done.2
  2.7 154.4 %shard_map.111 = (bf16[16,4,8,2048]{3,2,1,0:T(8,128)(2,1)}, bf16[4,2,128,1024]{3,2,1,0:T(8,128)(2,1)}, bf16[4,2,128,1024]{3,2,1,0:T(8,128)(2,1)}, bf16[4,2,128,1...) custom-call(s32[2,256]{1,0:T(2,128)} %bitcast.15, ...), custom_call_target="tpu_custom_call" | custom-call | tf_op jit(solution)/shard_map/pallas_call | solution.py:230
  157.2 0.0 copy-start
  157.2 1.6 copy-done
  158.8 0.0 copy-start.1
  158.8 1.6 copy-done.1
  160.4 17.3 %shard_map.112 = (bf16[256,2048]{1,0:T(8,128)(2,1)}, bf16[4,1024,1024]{2,1,0:T(8,128)(2,1)}, bf16[4,1024,1024]{2,1,0:T(8,128)(2,1)}, bf16[4,1024,1024]{2,1,0:T(8,128)(2,1)}) custom-call(s32[256,2]{1,0:T(8,128)S(1)} %copy.16.pos, bf16[512,2048]{1,0:T(8,128)(2,1)S(1)} %bitcast.9, bf16[4,256,1024]{2,1,0:T(8,128)(2,1)S(1)} %bitcast.10, ...), custom_call_target="tpu_custom_call" | custom-call | tf_op jit(solution)/shard_map/pallas_call | solution.py:273
Async XLA Ops:
  1.3 1.4 copy-start.2
  157.2 1.6 copy-start
  158.8 1.6 copy-start.1
